TPU v7x, 32 devices: a whole 2x2x4 slice. The times are simulated.
32 devices in a mesh: fsdp: 8 (over z, x), rep: 4 (over y, core).
Axes of the slice: x: 2, y: 2, z: 4, core: 2. Of those that a mesh axis runs over, the one named last changes fastest.
Arguments:
- layer_input: bfloat16 [32768, 768], P(('fsdp', 'rep')), may hold values from -6 to 6
- qkv_weight: bfloat16 [768, 2304], P('fsdp'), may hold values from -0.21875 to 0.21875
- attn_weight: bfloat16 [768, 768], P('fsdp'), may hold values from -1.75 to 1.75
- wide_weight: bfloat16 [768, 2304], P('fsdp'), may hold values from -0.21875 to 0.21875
- narrow_weight: bfloat16 [768, 1152], P('fsdp'), may hold values from -0.375 to 0.375
- first_gain: bfloat16 [768], P('fsdp'), may hold values from 0.099609375 to 1.8984375
- second_gain: bfloat16 [768], P('fsdp'), may hold values from 0.099609375 to 1.8984375
- out_grad: bfloat16 [32768, 768], P(('fsdp', 'rep')), may hold values from -12 to 12
- token_seg: int32 [32768], P(('fsdp', 'rep')), may hold values from 0 to 255, as said below
- token_live: int32 [32768], P(('fsdp', 'rep')), may hold values from 0 to 1, as said below
Outputs:
- layer_output: bfloat16 [32768, 768], P(('fsdp', 'rep'))
- input_grad: float32 [32768, 768], P(('fsdp', 'rep'))
- qkv_grad: float32 [768, 2304], P('fsdp')
- attn_grad: float32 [768, 768], P('fsdp')
- wide_grad: float32 [768, 2304], P('fsdp')
- narrow_grad: float32 [768, 1152], P('fsdp')
- first_grad: float32 [768], P('fsdp')
- second_grad: float32 [768], P('fsdp')
Inputs may be any that keep to these rules, and one draw needn't show every extreme that they name: `token_seg`: numbers never fall along the slots; all slots of one number lie in one block of 1024 slots (one device's), and each number begins at a multiple of 128; every block begins a new number; the last tile of the last block begins a number of its own. `token_live`: within each number of token_seg the live slots come first and its first slot is live; in every draw one block of 1024 slots holds a single number with every slot live.
All inputs are finite; a program needn't handle non-finite values.
Results may differ from a plain program's by a relative error of at most 0.018.
Values may be sent and summed in bfloat16 or wider, within the bound.
A program may use at most 320 MiB of HBM per device.

v0:
```python
import math
import jax
import jax.numpy as jnp
from jax import lax
from jax.sharding import PartitionSpec as P

HDIM = 64
TILE = 128
QBLOCK = 512
rope_base = 160000.0
eps = 1e-05
masked_score = -1e30


def layer_norm(values, scales):
    center = values - jnp.mean(values, axis=-1, keepdims=True)
    spread = jnp.mean(center * center, axis=-1, keepdims=True)
    return center * lax.rsqrt(spread + eps) * scales


def rope_tables(seg_rows):
    length = seg_rows.shape[0]
    firsts = seg_rows[::TILE]
    before = jnp.sum((firsts[None, :] < seg_rows[:, None]).astype(jnp.int32), axis=1)
    places = jnp.arange(length, dtype=jnp.int32) - TILE * before
    freq_index = jnp.arange(HDIM // 2, dtype=jnp.float32)
    inverse = jnp.exp(freq_index * (-2.0 * math.log(rope_base) / HDIM))
    angles = places.astype(jnp.float32)[:, None] * inverse[None, :]
    angles = jnp.concatenate([angles, angles], axis=1)
    return (jnp.cos(angles)[:, None, :], jnp.sin(angles)[:, None, :])


def rotate(values, cos_tab, sin_tab):
    half_dim = values.shape[-1] // 2
    turned = jnp.concatenate([-values[..., half_dim:], values[..., :half_dim]], axis=-1)
    return values * cos_tab + turned * sin_tab


def rotate_back(grads, cos_tab, sin_tab):
    half_dim = grads.shape[-1] // 2
    sined = grads * sin_tab
    return grads * cos_tab + jnp.concatenate(
        [sined[..., half_dim:], -sined[..., :half_dim]], axis=-1
    )


def geglu(lifted):
    half_ff = lifted.shape[1] // 2
    return jax.nn.gelu(lifted[:, :half_ff], approximate=False) * lifted[:, half_ff:]


def block_scores(query_rows, keyset, seg_rows, token_seg, live_keys, scaling):
    raw = (
        jnp.einsum("qhd,khd->hqk", query_rows, keyset, preferred_element_type=jnp.float32) * scaling
    )
    allowed = (seg_rows[:, None] == token_seg[None, :]) & live_keys[None, :]
    return jnp.where(allowed[None], raw, masked_score)


def on_device(
    layer_input,
    qkv_weight,
    attn_weight,
    wide_weight,
    narrow_weight,
    first_gain,
    second_gain,
    out_grad,
    token_seg,
    token_live,
):
    length = layer_input.shape[0]
    model_width = layer_input.shape[1]
    head_count = model_width // HDIM
    scaling = 1.0 / math.sqrt(HDIM)
    qkv_full, attn_full, wide_full, narrow_full, gain_one, gain_two = (
        lax.all_gather(qkv_weight, "fsdp", axis=0, tiled=True),
        lax.all_gather(attn_weight, "fsdp", axis=0, tiled=True),
        lax.all_gather(wide_weight, "fsdp", axis=0, tiled=True),
        lax.all_gather(narrow_weight, "fsdp", axis=0, tiled=True),
        lax.all_gather(first_gain, "fsdp", axis=0, tiled=True),
        lax.all_gather(second_gain, "fsdp", axis=0, tiled=True),
    )
    scale_one = gain_one.astype(jnp.float32)
    scale_two = gain_two.astype(jnp.float32)
    residual_in = layer_input.astype(jnp.float32)
    live_keys = token_live > 0
    cos_tab, sin_tab = rope_tables(token_seg)
    normed_one = layer_norm(residual_in, scale_one).astype(jnp.bfloat16)
    packed = jnp.dot(normed_one, qkv_full, preferred_element_type=jnp.float32)
    queries = rotate(
        packed[:, :model_width].reshape(length, head_count, HDIM), cos_tab, sin_tab
    ).astype(jnp.bfloat16)
    keyset = rotate(
        packed[:, model_width : 2 * model_width].reshape(length, head_count, HDIM), cos_tab, sin_tab
    ).astype(jnp.bfloat16)
    valueset = packed[:, 2 * model_width :].reshape(length, head_count, HDIM).astype(jnp.bfloat16)
    mixed_list = []
    lse_list = []
    for begin_row in range(0, length, QBLOCK):
        seg_rows = token_seg[begin_row : begin_row + QBLOCK]
        scores = block_scores(
            queries[begin_row : begin_row + QBLOCK], keyset, seg_rows, token_seg, live_keys, scaling
        )
        top_score = jnp.max(scores, axis=-1, keepdims=True)
        expo = jnp.exp(scores - top_score)
        total = jnp.sum(expo, axis=-1, keepdims=True)
        probs = (expo / total).astype(jnp.bfloat16)
        lse_list.append(top_score + jnp.log(total))
        block_out = jnp.einsum("hqk,khd->qhd", probs, valueset, preferred_element_type=jnp.float32)
        mixed_list.append(block_out.reshape(QBLOCK, model_width).astype(jnp.bfloat16))
    mixed_rows = jnp.concatenate(mixed_list, axis=0)
    middle = residual_in + jnp.dot(mixed_rows, attn_full, preferred_element_type=jnp.float32)
    normed_two = layer_norm(middle, scale_two).astype(jnp.bfloat16)
    lifted = jnp.dot(normed_two, wide_full, preferred_element_type=jnp.float32)
    hidden = geglu(lifted).astype(jnp.bfloat16)
    layer_out = middle + jnp.einsum(
        "tf,df->td", hidden, narrow_full, preferred_element_type=jnp.float32
    )
    qkv_full, attn_full, wide_full, narrow_full, gain_one, gain_two = (
        lax.all_gather(qkv_weight, "fsdp", axis=0, tiled=True),
        lax.all_gather(attn_weight, "fsdp", axis=0, tiled=True),
        lax.all_gather(wide_weight, "fsdp", axis=0, tiled=True),
        lax.all_gather(narrow_weight, "fsdp", axis=0, tiled=True),
        lax.all_gather(first_gain, "fsdp", axis=0, tiled=True),
        lax.all_gather(second_gain, "fsdp", axis=0, tiled=True),
    )
    scale_one = gain_one.astype(jnp.float32)
    scale_two = gain_two.astype(jnp.float32)
    grad_top = out_grad.astype(jnp.float32) * token_live.astype(jnp.float32)[:, None]
    grad_top_low = grad_top.astype(jnp.bfloat16)
    narrow_term = jnp.einsum("td,tf->df", grad_top_low, hidden, preferred_element_type=jnp.float32)
    grad_hidden = jnp.dot(grad_top_low, narrow_full, preferred_element_type=jnp.float32)
    _, pull_gate = jax.vjp(geglu, lifted)
    grad_lifted = pull_gate(grad_hidden)[0].astype(jnp.bfloat16)
    wide_term = jnp.einsum("td,tf->df", normed_two, grad_lifted, preferred_element_type=jnp.float32)
    grad_norm_two = jnp.einsum(
        "tf,df->td", grad_lifted, wide_full, preferred_element_type=jnp.float32
    )
    _, pull_two = jax.vjp(layer_norm, middle, scale_two)
    grad_mid_ln, second_term = pull_two(grad_norm_two)
    grad_middle = grad_top + grad_mid_ln
    grad_middle_low = grad_middle.astype(jnp.bfloat16)
    attn_term = jnp.einsum(
        "td,te->de", mixed_rows, grad_middle_low, preferred_element_type=jnp.float32
    )
    grad_mixed = jnp.einsum(
        "te,de->td", grad_middle_low, attn_full, preferred_element_type=jnp.float32
    )
    grad_mixed = grad_mixed.astype(jnp.bfloat16).reshape(length, head_count, HDIM)
    grad_keys = jnp.zeros((length, head_count, HDIM), jnp.float32)
    grad_values = jnp.zeros((length, head_count, HDIM), jnp.float32)
    grad_query_list = []
    for block_index, begin_row in enumerate(range(0, length, QBLOCK)):
        seg_rows = token_seg[begin_row : begin_row + QBLOCK]
        query_rows = queries[begin_row : begin_row + QBLOCK]
        grad_rows = grad_mixed[begin_row : begin_row + QBLOCK]
        scores = block_scores(query_rows, keyset, seg_rows, token_seg, live_keys, scaling)
        probs_f32 = jnp.exp(scores - lse_list[block_index])
        probs_low = probs_f32.astype(jnp.bfloat16)
        grad_values = grad_values + jnp.einsum(
            "hqk,qhd->khd", probs_low, grad_rows, preferred_element_type=jnp.float32
        )
        grad_probs = jnp.einsum(
            "qhd,khd->hqk", grad_rows, valueset, preferred_element_type=jnp.float32
        )
        row_delta = jnp.sum(probs_f32 * grad_probs, axis=-1, keepdims=True)
        grad_scores = (probs_f32 * (grad_probs - row_delta)).astype(jnp.bfloat16)
        grad_query_list.append(
            jnp.einsum("hqk,khd->qhd", grad_scores, keyset, preferred_element_type=jnp.float32)
            * scaling
        )
        grad_keys = (
            grad_keys
            + jnp.einsum(
                "hqk,qhd->khd", grad_scores, query_rows, preferred_element_type=jnp.float32
            )
            * scaling
        )
    grad_queries = jnp.concatenate(grad_query_list, axis=0)
    grad_packed = jnp.concatenate(
        [
            rotate_back(grad_queries, cos_tab, sin_tab).reshape(length, model_width),
            rotate_back(grad_keys, cos_tab, sin_tab).reshape(length, model_width),
            grad_values.reshape(length, model_width),
        ],
        axis=1,
    ).astype(jnp.bfloat16)
    qkv_term = jnp.einsum("td,tf->df", normed_one, grad_packed, preferred_element_type=jnp.float32)
    grad_norm_one = jnp.einsum(
        "tf,df->td", grad_packed, qkv_full, preferred_element_type=jnp.float32
    )
    _, pull_one = jax.vjp(layer_norm, residual_in, scale_one)
    grad_in_ln, first_term = pull_one(grad_norm_one)
    input_grad = grad_middle + grad_in_ln
    shares = (
        lax.psum_scatter(qkv_term, "fsdp", scatter_dimension=0, tiled=True),
        lax.psum_scatter(attn_term, "fsdp", scatter_dimension=0, tiled=True),
        lax.psum_scatter(wide_term, "fsdp", scatter_dimension=0, tiled=True),
        lax.psum_scatter(narrow_term, "fsdp", scatter_dimension=0, tiled=True),
        lax.psum_scatter(first_term, "fsdp", scatter_dimension=0, tiled=True),
        lax.psum_scatter(second_term, "fsdp", scatter_dimension=0, tiled=True),
    )
    shares = (
        lax.psum(shares[0].astype(jnp.bfloat16), "rep").astype(jnp.float32),
        lax.psum(shares[1].astype(jnp.bfloat16), "rep").astype(jnp.float32),
        lax.psum(shares[2].astype(jnp.bfloat16), "rep").astype(jnp.float32),
        lax.psum(shares[3].astype(jnp.bfloat16), "rep").astype(jnp.float32),
        lax.psum(shares[4].astype(jnp.bfloat16), "rep").astype(jnp.float32),
        lax.psum(shares[5].astype(jnp.bfloat16), "rep").astype(jnp.float32),
    )
    return (
        layer_out.astype(jnp.bfloat16),
        input_grad,
        shares[0],
        shares[1],
        shares[2],
        shares[3],
        shares[4],
        shares[5],
    )


def solution(mesh):
    return jax.shard_map(
        on_device,
        mesh=mesh,
        in_specs=(
            P(("fsdp", "rep"), None),
            P("fsdp", None),
            P("fsdp", None),
            P("fsdp", None),
            P("fsdp", None),
            P("fsdp"),
            P("fsdp"),
            P(("fsdp", "rep"), None),
            P(("fsdp", "rep")),
            P(("fsdp", "rep")),
        ),
        out_specs=(
            P(("fsdp", "rep"), None),
            P(("fsdp", "rep"), None),
            P("fsdp", None),
            P("fsdp", None),
            P("fsdp", None),
            P("fsdp", None),
            P("fsdp"),
            P("fsdp"),
        ),
        check_vma=False,
    )
```

profile of v0, /device:TPU:0, one launch (start us, length us, event | category | flops | bytes accessed | tf_op | source)
XLA Modules:
  0.0 737.4 jit_solution(18001098060533873576)
XLA Ops:
  13.6 1.3 fusion.91
  17.2 23.5 %all-reduce.7 = (bf16[768]{0:T(1024)(128)(2,1)S(1)}, bf16[768]{0:T(1024)(128)(2,1)S(1)}) all-reduce(bf16[768]{0:T(1024)(128)(2,1)S(1)} %dynamic-update-slice, bf16[768]{0:T(1024)(128)(2,1)S(1)} %dynamic-update-slice.1), channel_id=1, replica_groups=mesh['fsdp'=8,'rep'=4] {'fsdp'}, use_global_device_ids=true, to_apply=%add.2 | all-reduce | flops 1536 | bytes 6144
  42.2 1.7 broadcast_multiply_fusion.1
  46.7 1.6 copy.54
  48.3 1.7 compare_and_fusion.1
  50.0 28.4 %all-gather.5.cloned.1.call-done = bf16[768,2304]{1,0:T(8,128)(2,1)} async-done(((bf16[96,2304]{1,0:T(8,128)(2,1)}), bf16[768,2304]{1,0:T(8,128)(2,1)}) %all-gather.5.cloned.1.call-update) | async-done | bytes 3538960 | tf_op jit(solution)/shard_map/all_gather | solution.py:77
  78.4 6.2 fusion.63
  84.6 1.3 slice.141
  85.9 3.1 fusion.86
  89.0 3.6 copy.51
  92.5 1.7 copy.50
  94.3 3.5 copy.52
  97.8 2.4 slice_negate_fusion.2
  101.1 1.4 copy-done.6
  102.5 1.9 fusion.32
  104.4 10.9 %fusion.13 = (f32[12,512]{1,0:T(8,128)S(1)}, f32[12,512,1024]{2,1,0:T(8,128)}) fusion(pred[512,1024]{1,0:T(8,128)(4,1)S(1)} %copy-done.16, bf16[1024,12,64]{0,2,1:T(8,128)(2,1)S(1)} %get-tuple-element.73, bf16[1024,12,64]{0,2,1:T(8,128)(2,1)S(1)} %get-tuple-element.72), kind=kOutput, calls=%fused_computation.24 | convolution fusion | flops 824174592 | bytes 28073984 | tf_op jit(solution)/shard_map/qhd,khd->hqk/dot_general | solution.py:54
  115.4 10.7 %fusion.12 = (f32[12,512]{1,0:T(8,128)S(1)}, f32[12,512,1024]{2,1,0:T(8,128)}) fusion(pred[512,1024]{1,0:T(8,128)(4,1)S(1)} %copy-done.13, bf16[1024,12,64]{0,2,1:T(8,128)(2,1)S(1)} %get-tuple-element.73, bf16[1024,12,64]{0,2,1:T(8,128)(2,1)S(1)} %get-tuple-element.72), kind=kOutput, calls=%fused_computation.23 | convolution fusion | flops 824174592 | bytes 28073984 | tf_op jit(solution)/shard_map/qhd,khd->hqk/dot_general | solution.py:54
  126.1 12.1 %fusion.1 = f32[12,512]{1,0:T(8,128)S(1)} fusion(f32[12,512]{1,0:T(8,128)S(1)} %get-tuple-element.84, f32[12,512,1024]{2,1,0:T(8,128)} %get-tuple-element.85, pred[512,1024]{1,0:T(8,128)(4,1)S(1)} %copy-done.16), kind=kLoop, calls=%fused_computation.13 | loop fusion | flops 25159680 | bytes 25739264 | tf_op jit(solution)/shard_map/reduce_sum | solution.py:107
  138.2 13.8 %fusion.45 = bf16[12,64,512]{2,1,0:T(8,128)(2,1)} fusion(bf16[1024,12,64]{0,2,1:T(8,128)(2,1)S(1)} %bitcast.68, f32[12,512]{1,0:T(8,128)S(1)} %fusion.1, f32[12,512]{1,0:T(8,128)S(1)} %get-tuple-element.84, f32[12,512,1024]{2,1,0:T(8,128)} %get-tuple-element.85, pred[512,1024]{1,0:T(8,128)(4,1)S(1)} %copy-done.16), kind=kOutput, calls=%fused_computation.101 | convolution fusion | flops 837156864 | bytes 28098560 | tf_op jit(solution)/shard_map/hqk,khd->qhd/dot_general | solution.py:110
  153.0 1.4 slice-done.5
  154.4 7.3 fusion
  161.7 8.6 %fusion.46 = bf16[12,64,512]{2,1,0:T(8,128)(2,1)} fusion(bf16[1024,12,64]{0,2,1:T(8,128)(2,1)S(1)} %bitcast.69, f32[12,512]{1,0:T(8,128)S(1)} %fusion, f32[12,512]{1,0:T(8,128)S(1)} %get-tuple-element.86, f32[12,512,1024]{2,1,0:T(8,128)S(1)} %bitcast.61, pred[512,1024]{1,0:T(8,128)(4,1)S(1)} %copy-done.13), kind=kOutput, calls=%fused_computation.102 | convolution fusion | flops 837156864 | bytes 28098560 | tf_op jit(solution)/shard_map/hqk,khd->qhd/dot_general | solution.py:110
  170.3 3.3 fusion.92
  175.3 11.1 %all-gather.9.cloned.1.call-done = bf16[768,2304]{1,0:T(8,128)(2,1)} async-done(((bf16[96,2304]{1,0:T(8,128)(2,1)}), bf16[768,2304]{1,0:T(8,128)(2,1)}) %all-gather.9.cloned.1.call-update) | async-done | bytes 3538960 | tf_op jit(solution)/shard_map/all_gather | solution.py:79
  186.4 10.6 %fusion.83 = f32[1024,2304]{1,0:T(8,128)} fusion(bf16[768,2304]{1,0:T(8,128)(2,1)} %all-gather.9.cloned.1.call-done, f32[1024,768]{0,1:T(8,128)} %copy-done.19, f32[768]{0:T(1024)S(1)} %copy-done.53, f32[1024]{0:T(1024)S(1)} %fusion.68, f32[1024]{0:T(1024)S(1)} %broadcast_multiply_fusion.3), kind=kOutput, calls=%fused_computation.155 | convolution fusion | flops 3627024384 | bytes 16133120 | tf_op jit(solution)/shard_map/dot_general | solution.py:115
  197.0 35.9 %all-gather.11.cloned.1.call-done = bf16[768,1152]{1,0:T(8,128)(2,1)} async-done(((bf16[96,1152]{1,0:T(8,128)(2,1)}), bf16[768,1152]{1,0:T(8,128)(2,1)}) %all-gather.11.cloned.1.call-update) | async-done | bytes 1769488 | tf_op jit(solution)/shard_map/all_gather | solution.py:80
  232.9 15.2 %fusion.44 = (f32[1024,1152]{1,0:T(8,128)}, f32[1024,1152]{1,0:T(8,128)S(1)}, f32[1024,1152]{1,0:T(8,128)S(1)}) fusion(f32[1024,2304]{1,0:T(8,128)} %fusion.83, bf16[768,1152]{1,0:T(8,128)(2,1)} %all-gather.11.cloned.1.call-done, bf16[1024,768]{0,1:T(8,128)(2,1)S(1)} %copy-done.9, f32[1024]{0:T(1024)S(1)} %copy-done.42), kind=kOutput, calls=%fused_computation.98 | convolution fusion | flops 1890975744 | bytes 22220800 | tf_op jit(solution)/shard_map/dot_general | solution.py:133
  248.0 3.5 multiply_add_fusion
  251.6 9.5 %multiply_reduce_fusion.2 = (f32[768]{0:T(1024)}, f32[1024]{0:T(1024)S(1)}, f32[1024,768]{0,1:T(8,128)S(1)}) fusion(f32[1024,768]{0,1:T(8,128)S(1)} %copy-done.20, f32[1024]{0:T(1024)S(1)} %fusion.68, f32[1024]{0:T(1024)S(1)} %broadcast_multiply_fusion.3, f32[768]{0:T(1024)S(1)} %copy-done.53, bf16[768,2304]{1,0:T(8,128)(2,1)} %all-gather.9.cloned.1.call-done, ...), kind=kOutput, calls=%fused_computation.76 | convolution fusion | flops 3634100480 | bytes 19286016 | tf_op jit(solution)/shard_map/tf,df->td/dot_general | solution.py:137
  264.8 2.9 fusion.51
  267.7 5.7 fusion.47
  273.5 3.3 convolution_convert_fusion
  279.3 9.1 %fusion.59 = f32[768,2304]{1,0:T(8,128)} fusion(f32[1024,1152]{1,0:T(8,128)S(1)} %bitcast.77, f32[1024,1152]{1,0:T(8,128)} %get-tuple-element.56, f32[1024,768]{0,1:T(8,128)S(1)} %copy-done.21, f32[768]{0:T(1024)S(1)} %copy-done.53, f32[1024]{0:T(1024)S(1)} %fusion.68, f32[1024]{0:T(1024)S(1)} %broadcast_multiply_fusion.3), kind=kOutput, calls=%fused_computation.113 | convolution fusion | flops 3631742976 | bytes 19672064 | tf_op jit(solution)/shard_map/td,tf->df/dot_general | solution.py:136
  289.5 18.0 %multiply_reduce_fusion.1 = (f32[12,512]{1,0:T(8,128)S(1)}, f32[12,512,1024]{2,1,0:T(8,128)}) fusion(f32[12,512]{1,0:T(8,128)S(1)} %log_add_fusion.1, f32[12,512,1024]{2,1,0:T(8,128)} %get-tuple-element.87, pred[512,1024]{1,0:T(8,128)(4,1)S(1)} %copy-done.14, bf16[512,12,64]{0,2,1:T(8,128)(2,1)} %bitcast.78, bf16[1024,12,64]{0,2,1:T(8,128)(2,1)S(1)} %bitcast.70), kind=kOutput, calls=%fused_computation.4 | convolution fusion | flops 836757504 | bytes 53264384 | tf_op jit(solution)/shard_map/qhd,khd->hqk/dot_general | solution.py:164
  307.5 17.8 %multiply_reduce_fusion = (f32[12,512]{1,0:T(8,128)S(1)}, f32[12,512,1024]{2,1,0:T(8,128)}) fusion(f32[12,512]{1,0:T(8,128)S(1)} %log_add_fusion, f32[12,512,1024]{2,1,0:T(8,128)} %get-tuple-element.85, pred[512,1024]{1,0:T(8,128)(4,1)S(1)} %copy-done.17, bf16[512,12,64]{0,2,1:T(8,128)(2,1)} %bitcast.80, bf16[1024,12,64]{0,2,1:T(8,128)(2,1)S(1)} %bitcast.71), kind=kOutput, calls=%fused_computation.1 | convolution fusion | flops 836757504 | bytes 53264384 | tf_op jit(solution)/shard_map/qhd,khd->hqk/dot_general | solution.py:164
  325.4 42.7 %multiply_convert_fusion = (bf16[12,512,1024]{2,1,0:T(8,128)(2,1)}, bf16[12,512,1024]{2,1,0:T(8,128)(2,1)}) fusion(f32[12,512,1024]{2,1,0:T(8,128)} %get-tuple-element.95, f32[12,512]{1,0:T(8,128)S(1)} %get-tuple-element.94, f32[12,512]{1,0:T(8,128)S(1)} %log_add_fusion, f32[12,512,1024]{2,1,0:T(8,128)} %get-tuple-element.85, ...), kind=kLoop, calls=%fused_computation | loop fusion | flops 75497472 | bytes 126976000 | tf_op jit(solution)/shard_map/convert_element_type | solution.py:168
  368.1 10.4 %convolution_multiply_fusion = f32[12,64,512]{2,1,0:T(8,128)} fusion(bf16[1024,12,64]{0,2,1:T(8,128)(2,1)} %copy-done.3, bf16[12,512,1024]{2,1,0:T(8,128)(2,1)} %get-tuple-element.100), kind=kOutput, calls=%fused_computation.99 | convolution fusion | flops 805699584 | bytes 15728640 | tf_op jit(solution)/shard_map/hqk,khd->qhd/dot_general | solution.py:170
  378.5 6.6 convolution_multiply_fusion.1
  385.1 2.3 maximum_multiply_fusion.3
  389.6 2.1 fusion.36
  391.7 2.3 fusion.55
  395.5 3.7 bitcast_multiply_fusion
  401.6 12.1 %fusion.4 = f32[12,64,1024]{2,1,0:T(8,128)S(1)} fusion(bf16[512,12,64]{0,2,1:T(8,128)(2,1)S(1)} %bitcast.81, f32[12,512]{1,0:T(8,128)S(1)} %log_add_fusion, f32[12,512,1024]{2,1,0:T(8,128)} %get-tuple-element.85, pred[512,1024]{1,0:T(8,128)(4,1)S(1)} %copy-done.18), kind=kOutput, calls=%fused_computation.16 | convolution fusion | flops 830472192 | bytes 29646848 | tf_op jit(solution)/shard_map/hqk,qhd->khd/dot_general | solution.py:161
  413.7 12.0 %add_convert_fusion.1 = bf16[12,64,1024]{2,1,0:T(8,128)(2,1)S(1)} fusion(f32[12,64,1024]{2,1,0:T(8,128)S(1)} %fusion.4, bf16[512,12,64]{0,2,1:T(8,128)(2,1)S(1)} %bitcast.79, f32[12,512]{1,0:T(8,128)S(1)} %log_add_fusion.1, f32[12,512,1024]{2,1,0:T(8,128)} %get-tuple-element.87, pred[512,1024]{1,0:T(8,128)(4,1)S(1)} %copy-done.15), kind=kOutput, calls=%fused_computation.78 | convolution fusion | flops 832045056 | bytes 31219712 | tf_op jit(solution)/shard_map/hqk,qhd->khd/dot_general | solution.py:161
  426.9 6.8 fusion.39
  434.4 7.0 fusion.30
  441.5 1.6 copy-done.23
  443.1 1.3 fusion.28
  444.5 3.4 add_convert_fusion.2
  447.9 1.6 convert_element_type.166
  449.5 1.7 convert_element_type.170
  451.2 98.6 %reduce-scatter.9.cloned.1.call-done = f32[96,2304]{1,0:T(8,128)} async-done(((f32[768,2304]{1,0:T(8,128)}), f32[96,2304]{1,0:T(8,128)}) %reduce-scatter.9.cloned.1.call-update) | async-done | bytes 884752 | tf_op jit(solution)/shard_map/reduce_scatter | solution.py:199
  549.8 2.0 convert_element_type.168
  551.8 130.2 %reduce-scatter.5.cloned.1.call-done = f32[96,2304]{1,0:T(8,128)} async-done(((f32[768,2304]{1,0:T(8,128)}), f32[96,2304]{1,0:T(8,128)}) %reduce-scatter.5.cloned.1.call-update) | async-done | bytes 884752 | tf_op jit(solution)/shard_map/reduce_scatter | solution.py:197
  682.0 2.0 convert_element_type.164
  684.0 2.6 copy.55
  686.6 19.7 %all-reduce.6 = (bf16[768]{0:T(1024)(128)(2,1)S(1)}, bf16[768]{0:T(1024)(128)(2,1)S(1)}) all-reduce(f32[768]{0:T(1024)S(1)} %get-tuple-element.42, f32[768]{0:T(1024)S(1)} %copy-done.54), channel_id=6, replica_groups=mesh['fsdp'=8,'rep'=4] {'fsdp'}, use_global_device_ids=true, to_apply=%region_24.25.clone | all-reduce | flops 1536 | bytes 9216
  706.5 5.6 all-reduce.8
  713.1 6.1 add_add_fusion.2
  719.2 3.6 copy.56
  723.3 1.6 convert_element_type.167
  724.9 2.0 convert_element_type.165
  726.9 1.7 convert_element_type.171
  728.7 2.0 convert_element_type.169
  (202 shorter events, 32.0 us)
Async XLA Ops:
  7.2 36.7 %copy-start.34 = (bf16[1024,768]{1,0:T(8,128)(2,1)S(1)}, bf16[1024,768]{1,0:T(8,128)(2,1)}, u32[]{:S(2)}) copy-start(bf16[1024,768]{1,0:T(8,128)(2,1)} %param.10) | copy-start | bytes 4718596
  7.2 71.2 %all-gather.5.cloned.1.call-start = ((), (), s32[]{:S(2)}) async-start(), calls=%async_computation.4 | async-start | bytes 3981312 | tf_op jit(solution)/shard_map/all_gather | solution.py:77
  7.9 162.4 %all-gather.7.cloned.1.call-start = ((), (), s32[]{:S(2)}) async-start(), calls=%async_computation.5 | async-start | bytes 1327104 | tf_op jit(solution)/shard_map/all_gather | solution.py:78
  8.7 177.7 %all-gather.9.cloned.1.call-start = ((), (), s32[]{:S(2)}) async-start(), calls=%async_computation.6 | async-start | bytes 3981312 | tf_op jit(solution)/shard_map/all_gather | solution.py:79
  9.4 223.5 %all-gather.11.cloned.1.call-start = ((), (), s32[]{:S(2)}) async-start(), calls=%async_computation.7 | async-start | bytes 1990656 | tf_op jit(solution)/shard_map/all_gather | solution.py:80
  10.0 437.9 %reduce-scatter.7.cloned.1.call-start = ((), (), s32[]{:S(2)}) async-start(), calls=%async_computation.9 | async-start | bytes 2654208 | tf_op jit(solution)/shard_map/reduce_scatter | solution.py:198
  40.7 37.7 %copy-start.44 = (f32[768]{0:T(1024)}, f32[768]{0:T(1024)S(1)}, u32[]{:S(2)}) copy-start(f32[768]{0:T(1024)S(1)} %convert_element_type.135) | copy-start | bytes 9220
  43.9 57.2 %copy-start.29 = (f32[1024,64]{0,1:T(8,128)}, f32[1024,64]{0,1:T(8,128)S(1)}, u32[]{:S(2)}) copy-start(f32[1024,64]{0,1:T(8,128)S(1)} %get-tuple-element.77) | copy-start | bytes 786436
  44.7 125.7 %copy-start.1 = (bf16[1024,768]{0,1:T(8,128)(2,1)}, bf16[1024,768]{0,1:T(8,128)(2,1)S(1)}, u32[]{:S(2)}) copy-start(bf16[1024,768]{0,1:T(8,128)(2,1)S(1)} %copy.49) | copy-start | bytes 4718596
  44.7 2.0 copy-start.35
  44.7 3.6 copy-start.52
  45.0 39.6 %copy-start.40 = (f32[1024]{0:T(1024)}, f32[1024]{0:T(1024)S(1)}, u32[]{:S(2)}) copy-start(f32[1024]{0:T(1024)S(1)} %broadcast_multiply_fusion.4) | copy-start | bytes 12292
  46.6 38.0 %copy-start.46 = (f32[1024]{0:T(1024)}, f32[1024]{0:T(1024)S(1)}, u32[]{:S(2)}) copy-start(f32[1024]{0:T(1024)S(1)} %fusion.67) | copy-start | bytes 12292
  97.8 2.8 copy-start.5
  100.6 1.9 copy-start.6
  100.6 1.9 copy-start.31
  104.4 11.0 %copy-start.3 = (bf16[1024,12,64]{0,2,1:T(8,128)(2,1)}, bf16[1024,12,64]{0,2,1:T(8,128)(2,1)S(1)}, u32[]{:S(2)}) copy-start(bf16[1024,12,64]{0,2,1:T(8,128)(2,1)S(1)} %get-tuple-element.73) | copy-start | bytes 4718596
  104.4 11.0 %copy-start.7 = (bf16[1024,12,64]{0,2,1:T(8,128)(2,1)}, bf16[1024,12,64]{0,2,1:T(8,128)(2,1)S(1)}, u32[]{:S(2)}) copy-start(bf16[1024,12,64]{0,2,1:T(8,128)(2,1)S(1)} %get-tuple-element.72) | copy-start | bytes 4718596
  104.4 10.9 %copy-start.13 = (pred[512,1024]{1,0:T(8,128)(4,1)S(1)}, pred[512,1024]{1,0:T(8,128)(4,1)}, u32[]{:S(2)}) copy-start(pred[512,1024]{1,0:T(8,128)(4,1)} %get-tuple-element.78) | copy-start | bytes 1572868
  138.2 13.9 %slice-start = ((s8[25165824]{0:T(1024)(128)(4,1)}), s8[4194304]{0:T(1024)(128)(4,1)S(1)}, s32[]{:S(2)}) async-start(s8[25165824]{0:T(1024)(128)(4,1)} %bitcast.60), calls=%async_computation.13 | async-start | bytes 8388608
  138.2 13.8 %slice-start.1 = ((s8[25165824]{0:T(1024)(128)(4,1)}), s8[4194304]{0:T(1024)(128)(4,1)S(1)}, s32[]{:S(2)}) async-start(s8[25165824]{0:T(1024)(128)(4,1)} %bitcast.60), calls=%async_computation.14 | async-start | bytes 8388608
  138.2 13.8 %slice-start.2 = ((s8[25165824]{0:T(1024)(128)(4,1)}), s8[4194304]{0:T(1024)(128)(4,1)S(1)}, s32[]{:S(2)}) async-start(s8[25165824]{0:T(1024)(128)(4,1)} %bitcast.60), calls=%async_computation.15 | async-start | bytes 8388608
  138.2 13.8 %slice-start.3 = ((s8[25165824]{0:T(1024)(128)(4,1)}), s8[4194304]{0:T(1024)(128)(4,1)S(1)}, s32[]{:S(2)}) async-start(s8[25165824]{0:T(1024)(128)(4,1)} %bitcast.60), calls=%async_computation.16 | async-start | bytes 8388608
  138.2 14.8 %slice-start.4 = ((s8[25165824]{0:T(1024)(128)(4,1)}), s8[4194304]{0:T(1024)(128)(4,1)S(1)}, s32[]{:S(2)}) async-start(s8[25165824]{0:T(1024)(128)(4,1)} %bitcast.60), calls=%async_computation.17 | async-start | bytes 8388608
  138.2 16.1 %slice-start.5 = ((s8[25165824]{0:T(1024)(128)(4,1)}), s8[4194304]{0:T(1024)(128)(4,1)S(1)}, s32[]{:S(2)}) async-start(s8[25165824]{0:T(1024)(128)(4,1)} %bitcast.60), calls=%async_computation.18 | async-start | bytes 8388608
  173.6 12.7 %copy-start.53 = (f32[768]{0:T(1024)S(1)}, f32[768]{0:T(1024)}, u32[]{:S(2)}) copy-start(f32[768]{0:T(1024)} %convert_element_type.150) | copy-start | bytes 9220
  175.3 57.6 %copy-start.9 = (bf16[1024,768]{0,1:T(8,128)(2,1)S(1)}, bf16[1024,768]{0,1:T(8,128)(2,1)}, u32[]{:S(2)}) copy-start(bf16[1024,768]{0,1:T(8,128)(2,1)} %copy.54) | copy-start | bytes 4718596
  175.3 57.6 %copy-start.42 = (f32[1024]{0:T(1024)S(1)}, f32[1024]{0:T(1024)}, u32[]{:S(2)}) copy-start(f32[1024]{0:T(1024)} %convert_element_type.155) | copy-start | bytes 12292
  232.9 15.2 %copy-start.24 = (f32[1024,2304]{1,0:T(8,128)S(1)}, f32[1024,2304]{1,0:T(8,128)}, u32[]{:S(2)}) copy-start(f32[1024,2304]{1,0:T(8,128)} %fusion.83) | copy-start | bytes 28311556
  248.0 3.5 copy-start.20
  251.6 9.6 %copy-start.25 = (f32[1024,1152]{1,0:T(8,128)}, f32[1024,1152]{1,0:T(8,128)S(1)}, u32[]{:S(2)}) copy-start(f32[1024,1152]{1,0:T(8,128)S(1)} %get-tuple-element.58) | copy-start | bytes 14155780
  261.9 2.8 copy-start.57
  262.0 2.8 copy-start.58
  267.7 181.8 %reduce-scatter.11.cloned.1.call-start = ((), (), s32[]{:S(2)}) async-start(), calls=%async_computation.11 | async-start | bytes 3981312 | tf_op jit(solution)/shard_map/reduce_scatter | solution.py:200
  273.4 4.7 slice-start.9
  273.4 276.4 %reduce-scatter.9.cloned.1.call-start = ((), (), s32[]{:S(2)}) async-start(), calls=%async_computation.10 | async-start | bytes 7962624 | tf_op jit(solution)/shard_map/reduce_scatter | solution.py:199
  273.5 4.6 slice-start.10
  276.9 2.5 copy-start.21
  288.5 393.5 %reduce-scatter.5.cloned.1.call-start = ((), (), s32[]{:S(2)}) async-start(), calls=%async_computation.8 | async-start | bytes 7962624 | tf_op jit(solution)/shard_map/reduce_scatter | solution.py:197
  289.5 18.0 %copy-start.17 = (pred[512,1024]{1,0:T(8,128)(4,1)S(1)}, pred[512,1024]{1,0:T(8,128)(4,1)}, u32[]{:S(2)}) copy-start(pred[512,1024]{1,0:T(8,128)(4,1)} %get-tuple-element.79) | copy-start | bytes 1572868
  368.0 10.4 %copy-start = (bf16[12,512,1024]{2,1,0:T(8,128)(2,1)S(1)}, bf16[12,512,1024]{2,1,0:T(8,128)(2,1)}, u32[]{:S(2)}) copy-start(bf16[12,512,1024]{2,1,0:T(8,128)(2,1)} %get-tuple-element.101) | copy-start | bytes 37748740
  378.5 6.6 copy-start.32
  389.6 2.1 copy-start.8
  389.6 4.4 slice-start.6
  391.7 2.7 slice-start.7
  391.7 3.9 slice-start.8
  391.7 3.9 copy-start.28
  401.6 24.1 %copy-start.38 = (bf16[1024,12,64]{0,2,1:T(8,128)(2,1)}, bf16[1024,12,64]{0,2,1:T(8,128)(2,1)S(1)}, u32[]{:S(2)}) copy-start(bf16[1024,12,64]{0,2,1:T(8,128)(2,1)S(1)} %fusion.37) | copy-start | bytes 4718596
  401.6 12.1 %copy-start.15 = (pred[512,1024]{1,0:T(8,128)(4,1)S(1)}, pred[512,1024]{1,0:T(8,128)(4,1)}, u32[]{:S(2)}) copy-start(pred[512,1024]{1,0:T(8,128)(4,1)} %get-tuple-element.78) | copy-start | bytes 1572868
  401.6 12.1 %copy-start.26 = (bf16[512,768]{0,1:T(8,128)(2,1)S(1)}, bf16[512,768]{0,1:T(8,128)(2,1)}, u32[]{:S(2)}) copy-start(bf16[512,768]{0,1:T(8,128)(2,1)} %get-tuple-element.70) | copy-start | bytes 2359300
  413.7 13.2 %copy-start.2 = (bf16[1024,768]{0,1:T(8,128)(2,1)S(1)}, bf16[1024,768]{0,1:T(8,128)(2,1)}, u32[]{:S(2)}) copy-start(bf16[1024,768]{0,1:T(8,128)(2,1)} %copy-done.1) | copy-start | bytes 4718596
  413.7 13.2 %copy-start.37 = (bf16[1024,768]{0,1:T(8,128)(2,1)S(1)}, bf16[1024,768]{0,1:T(8,128)(2,1)}, u32[]{:S(2)}) copy-start(bf16[1024,768]{0,1:T(8,128)(2,1)} %fusion.36) | copy-start | bytes 4718596
  413.7 13.2 %copy-start.41 = (f32[1024]{0:T(1024)S(1)}, f32[1024]{0:T(1024)}, u32[]{:S(2)}) copy-start(f32[1024]{0:T(1024)} %copy-done.40) | copy-start | bytes 12292
  413.7 13.2 %copy-start.45 = (f32[768]{0:T(1024)S(1)}, f32[768]{0:T(1024)}, u32[]{:S(2)}) copy-start(f32[768]{0:T(1024)} %copy-done.44) | copy-start | bytes 9220
  413.7 13.1 %copy-start.47 = (f32[1024]{0:T(1024)S(1)}, f32[1024]{0:T(1024)}, u32[]{:S(2)}) copy-start(f32[1024]{0:T(1024)} %copy-done.46) | copy-start | bytes 12292
  433.7 289.6 %all-reduce.12.cloned.1.call-start = ((), (), s32[]{:S(2)}) async-start(), calls=%async_computation.12 | async-start | bytes 2506752 | tf_op jit(solution)/shard_map/psum | solution.py:205
  434.4 7.1 copy-start.51
  434.4 10.0 %copy-start.33 = (bf16[1024,1152]{1,0:T(8,128)(2,1)S(1)}, bf16[1024,1152]{1,0:T(8,128)(2,1)}, u32[]{:S(2)}) copy-start(bf16[1024,1152]{1,0:T(8,128)(2,1)} %get-tuple-element.59) | copy-start | bytes 7077892
  434.4 10.0 %copy-start.55 = (bf16[768,1152]{1,0:T(8,128)(2,1)S(1)}, bf16[768,1152]{1,0:T(8,128)(2,1)}, u32[]{:S(2)}) copy-start(bf16[768,1152]{1,0:T(8,128)(2,1)} %all-gather.11.cloned.1.call-done) | copy-start | bytes 5308420
  441.4 3.0 copy-start.22
  551.8 134.8 %copy-start.54 = (f32[768]{0:T(1024)S(1)}, f32[768]{0:T(1024)}, u32[]{:S(2)}) copy-start(f32[768]{0:T(1024)} %get-tuple-element.40) | copy-start | bytes 9220
  551.8 161.3 %copy-start.10 = (bf16[1024,768]{0,1:T(8,128)(2,1)S(1)}, bf16[1024,768]{0,1:T(8,128)(2,1)}, u32[]{:S(2)}) copy-start(bf16[1024,768]{0,1:T(8,128)(2,1)} %copy.54) | copy-start | bytes 4718596
  551.8 161.3 %copy-start.43 = (f32[1024]{0:T(1024)S(1)}, f32[1024]{0:T(1024)}, u32[]{:S(2)}) copy-start(f32[1024]{0:T(1024)} %convert_element_type.155) | copy-start | bytes 12292
  551.8 161.3 %copy-start.49 = (f32[1024]{0:T(1024)S(1)}, f32[1024]{0:T(1024)}, u32[]{:S(2)}) copy-start(f32[1024]{0:T(1024)} %copy-done.48) | copy-start | bytes 12292
  (15 other events, 21.3 us)
Sparse Core Ops, SparseCore 0:
  10.2 68.1 all-gather.4
  80.6 39.5 all-gather.6
  122.4 63.9 all-gather.8
  188.4 44.4 all-gather.10
  267.8 67.9 reduce-scatter.6
  339.3 78.1 reduce-scatter.10
  421.2 128.5 reduce-scatter.8
  553.9 128.0 reduce-scatter.4
  685.2 38.0 all-reduce.11
where the time goes:
time: 747 us; the launch traced here: 737 us
  waiting for transfers between devices  307 us (41%)
  matrix products  210 us (28%)
  other arithmetic  109 us (15%)
  blocking collectives  48.8 us (7%)
  local copies, waits for them, and re-layouts  45.4 us (6%)
  between operations  16.1 us (2%)
    reduce_scatter x1, waiting for transfers between devices, on_device(): lax.psum_scatter(qkv_term, 'fsdp', scatter_dimension=0, tiled=True)  130 us
    reduce_scatter x1, waiting for transfers between devices, on_device(): lax.psum_scatter(wide_term, 'fsdp', scatter_dimension=0, tiled=True)  98.6 us
    unnamed x2, blocking collectives  43.2 us
    convert_element_type x1, other arithmetic, on_device(): grad_scores = (probs_f32 * (grad_probs - row_delta)).astype(jnp.bfloat16)  42.7 us
    all_gather x1, waiting for transfers between devices, on_device(): lax.all_gather(narrow_weight, 'fsdp', axis=0, tiled=True)  35.9 us
    dot_general x2, matrix products, on_device(): jnp.einsum('qhd,khd->hqk', grad_rows, valueset, preferred_element_type=jn...  35.9 us
    unnamed x151, local copies, waits for them, and re-layouts  29.4 us
    all_gather x1, waiting for transfers between devices, on_device(): lax.all_gather(qkv_weight, 'fsdp', axis=0, tiled=True)  28.4 us
  transfers between devices with their start and end apart: 9, of which 6 were waited for; matrix products, arithmetic and copies ran while one was open for 41% of the time, Pallas kernels for 0%

commit v1 on v0

--- a/solution.py
+++ b/solution.py
@@ -10,6 +10,19 @@
 rope_base = 160000.0
 eps = 1e-05
 masked_score = -1e30
+
+
+def collect(shard, axis, dim):
+    length, place, width = (lax.axis_size(axis), lax.axis_index(axis), shard.shape[dim])
+    right = [(i, (i + 1) % length) for i in range(length)]
+    out = jnp.zeros((*shard.shape[:dim], length * width, *shard.shape[dim + 1 :]), shard.dtype)
+    held = shard
+    for turn in range(length):
+        source = (place - turn) % length
+        out = lax.dynamic_update_slice_in_dim(out, held, source * width, axis=dim)
+        if turn < length - 1:
+            held = lax.ppermute(held, axis, right)
+    return out
 
 
 def layer_norm(values, scales):
@@ -77,7 +90,7 @@
         lax.all_gather(qkv_weight, "fsdp", axis=0, tiled=True),
         lax.all_gather(attn_weight, "fsdp", axis=0, tiled=True),
         lax.all_gather(wide_weight, "fsdp", axis=0, tiled=True),
-        lax.all_gather(narrow_weight, "fsdp", axis=0, tiled=True),
+        collect(narrow_weight, "fsdp", 0),
         lax.all_gather(first_gain, "fsdp", axis=0, tiled=True),
         lax.all_gather(second_gain, "fsdp", axis=0, tiled=True),
     )

time: 747 us -> 780 us (1.044)
  waiting for transfers between devices: 307 us -> 339 us
    ppermute x0 -> x7, waiting for transfers between devices: none -> 93.6 us  [collect(): held = lax.ppermute(held, axis, right)]
    reduce_scatter x1, waiting for transfers between devices: 98.6 us -> 36.6 us  [on_device(): lax.psum_scatter(wide_term, 'fsdp', scatter_dimension=0, tiled=True)]
    unnamed x151 -> x155, local copies, waits for them, and re-layouts: 29.4 us -> 30.4 us
  transfers between devices with their start and end apart: 9 -> 16, of which waited for: 6 -> 13; matrix products, arithmetic and copies ran while one was open for 41% -> 40% of each run, Pallas kernels for 0% -> 0%
where the time goes in v1:
time: 780 us; the launch traced here: 771 us
  waiting for transfers between devices  339 us (43%)
  matrix products  208 us (27%)
  other arithmetic  109 us (14%)
  blocking collectives  48.8 us (6%)
  local copies, waits for them, and re-layouts  47.7 us (6%)
  between operations  16.1 us (2%)
    reduce_scatter x1, waiting for transfers between devices, on_device(): lax.psum_scatter(qkv_term, 'fsdp', scatter_dimension=0, tiled=True)  130 us
    ppermute x7, waiting for transfers between devices, collect(): held = lax.ppermute(held, axis, right)  93.6 us
    unnamed x2, blocking collectives  43.2 us
    convert_element_type x1, other arithmetic, on_device(): grad_scores = (probs_f32 * (grad_probs - row_delta)).astype(jnp.bfloat16)  42.6 us
    reduce_scatter x1, waiting for transfers between devices, on_device(): lax.psum_scatter(wide_term, 'fsdp', scatter_dimension=0, tiled=True)  36.6 us
    all_gather x1, waiting for transfers between devices, on_device(): lax.all_gather(narrow_weight, 'fsdp', axis=0, tiled=True)  35.8 us
    dot_general x2, matrix products, on_device(): jnp.einsum('qhd,khd->hqk', grad_rows, valueset, preferred_element_type=jn...  35.8 us
    unnamed x155, local copies, waits for them, and re-layouts  30.4 us
  transfers between devices with their start and end apart: 16, of which 13 were waited for; matrix products, arithmetic and copies ran while one was open for 40% of the time, Pallas kernels for 0%

profile of v1, /device:TPU:0, one launch (start us, length us, event | category | flops | bytes accessed | tf_op | source)
XLA Modules:
  0.0 770.5 jit_solution(3531391745146600196)
XLA Ops:
  17.2 23.5 %all-reduce.7 = (bf16[768]{0:T(1024)(128)(2,1)S(1)}, bf16[768]{0:T(1024)(128)(2,1)S(1)}) all-reduce(bf16[768]{0:T(1024)(128)(2,1)S(1)} %dynamic-update-slice, bf16[768]{0:T(1024)(128)(2,1)S(1)} %dynamic-update-slice.1), channel_id=1, replica_groups=mesh['fsdp'=8,'rep'=4] {'fsdp'}, use_global_device_ids=true, to_apply=%add.2 | all-reduce | flops 1536 | bytes 6144
  42.2 1.7 broadcast_multiply_fusion.1
  48.3 1.7 compare_and_fusion.1
  50.0 28.4 %all-gather.5.cloned.1.call-done = bf16[768,2304]{1,0:T(8,128)(2,1)} async-done(((bf16[96,2304]{1,0:T(8,128)(2,1)}), bf16[768,2304]{1,0:T(8,128)(2,1)}) %all-gather.5.cloned.1.call-update) | async-done | bytes 3538960 | tf_op jit(solution)/shard_map/all_gather | solution.py:90
  78.4 6.2 fusion.63
  85.9 3.1 fusion.86
  89.0 3.6 copy.51
  92.5 1.7 copy.50
  94.3 3.5 copy.52
  97.8 2.4 slice_negate_fusion.2
  102.5 1.9 fusion.32
  104.4 10.8 %fusion.13 = (f32[12,512]{1,0:T(8,128)S(1)}, f32[12,512,1024]{2,1,0:T(8,128)}) fusion(pred[512,1024]{1,0:T(8,128)(4,1)S(1)} %copy-done.16, bf16[1024,12,64]{0,2,1:T(8,128)(2,1)S(1)} %get-tuple-element.73, bf16[1024,12,64]{0,2,1:T(8,128)(2,1)S(1)} %get-tuple-element.72), kind=kOutput, calls=%fused_computation.24 | convolution fusion | flops 824174592 | bytes 28073984 | tf_op jit(solution)/shard_map/qhd,khd->hqk/dot_general | solution.py:67
  115.3 10.7 %fusion.12 = (f32[12,512]{1,0:T(8,128)S(1)}, f32[12,512,1024]{2,1,0:T(8,128)}) fusion(pred[512,1024]{1,0:T(8,128)(4,1)S(1)} %copy-done.13, bf16[1024,12,64]{0,2,1:T(8,128)(2,1)S(1)} %get-tuple-element.73, bf16[1024,12,64]{0,2,1:T(8,128)(2,1)S(1)} %get-tuple-element.72), kind=kOutput, calls=%fused_computation.23 | convolution fusion | flops 824174592 | bytes 28073984 | tf_op jit(solution)/shard_map/qhd,khd->hqk/dot_general | solution.py:67
  126.0 12.0 %fusion.1 = f32[12,512]{1,0:T(8,128)S(1)} fusion(f32[12,512]{1,0:T(8,128)S(1)} %get-tuple-element.84, f32[12,512,1024]{2,1,0:T(8,128)} %get-tuple-element.85, pred[512,1024]{1,0:T(8,128)(4,1)S(1)} %copy-done.16), kind=kLoop, calls=%fused_computation.13 | loop fusion | flops 25159680 | bytes 25739264 | tf_op jit(solution)/shard_map/reduce_sum | solution.py:120
  138.1 13.8 %fusion.45 = bf16[12,64,512]{2,1,0:T(8,128)(2,1)} fusion(bf16[1024,12,64]{0,2,1:T(8,128)(2,1)S(1)} %bitcast.68, f32[12,512]{1,0:T(8,128)S(1)} %fusion.1, f32[12,512]{1,0:T(8,128)S(1)} %get-tuple-element.84, f32[12,512,1024]{2,1,0:T(8,128)} %get-tuple-element.85, pred[512,1024]{1,0:T(8,128)(4,1)S(1)} %copy-done.16), kind=kOutput, calls=%fused_computation.101 | convolution fusion | flops 837156864 | bytes 28098560 | tf_op jit(solution)/shard_map/hqk,khd->qhd/dot_general | solution.py:123
  154.2 7.3 fusion
  161.5 8.7 %fusion.46 = bf16[12,64,512]{2,1,0:T(8,128)(2,1)} fusion(bf16[1024,12,64]{0,2,1:T(8,128)(2,1)S(1)} %bitcast.69, f32[12,512]{1,0:T(8,128)S(1)} %fusion, f32[12,512]{1,0:T(8,128)S(1)} %get-tuple-element.86, f32[12,512,1024]{2,1,0:T(8,128)S(1)} %bitcast.61, pred[512,1024]{1,0:T(8,128)(4,1)S(1)} %copy-done.13), kind=kOutput, calls=%fused_computation.102 | convolution fusion | flops 837156864 | bytes 28098560 | tf_op jit(solution)/shard_map/hqk,khd->qhd/dot_general | solution.py:123
  170.2 3.3 fusion.92
  175.2 11.2 %all-gather.9.cloned.1.call-done = bf16[768,2304]{1,0:T(8,128)(2,1)} async-done(((bf16[96,2304]{1,0:T(8,128)(2,1)}), bf16[768,2304]{1,0:T(8,128)(2,1)}) %all-gather.9.cloned.1.call-update) | async-done | bytes 3538960 | tf_op jit(solution)/shard_map/all_gather | solution.py:92
  186.4 10.6 %fusion.83 = f32[1024,2304]{1,0:T(8,128)} fusion(bf16[768,2304]{1,0:T(8,128)(2,1)} %all-gather.9.cloned.1.call-done, f32[1024,768]{0,1:T(8,128)} %copy-done.19, f32[768]{0:T(1024)S(1)} %copy-done.55, f32[1024]{0:T(1024)S(1)} %fusion.68, f32[1024]{0:T(1024)S(1)} %broadcast_multiply_fusion.3), kind=kOutput, calls=%fused_computation.163 | convolution fusion | flops 3627024384 | bytes 16133120 | tf_op jit(solution)/shard_map/dot_general | solution.py:128
  197.0 35.8 %all-gather.11.cloned.1.call-done = bf16[768,1152]{1,0:T(8,128)(2,1)} async-done(((bf16[96,1152]{1,0:T(8,128)(2,1)}), bf16[768,1152]{1,0:T(8,128)(2,1)}) %all-gather.11.cloned.1.call-update) | async-done | bytes 1769488 | tf_op jit(solution)/shard_map/all_gather | solution.py:137
  232.9 15.2 %fusion.44 = (f32[1024,1152]{1,0:T(8,128)}, f32[1024,1152]{1,0:T(8,128)S(1)}, f32[1024,1152]{1,0:T(8,128)S(1)}) fusion(f32[1024,2304]{1,0:T(8,128)} %fusion.83, bf16[768,1152]{1,0:T(8,128)(2,1)} %all-gather.11.cloned.1.call-done, bf16[1024,768]{0,1:T(8,128)(2,1)S(1)} %copy-done.9, f32[1024]{0:T(1024)S(1)} %copy-done.44), kind=kOutput, calls=%fused_computation.98 | convolution fusion | flops 1890975744 | bytes 22220800 | tf_op jit(solution)/shard_map/dot_general | solution.py:146
  248.0 3.5 multiply_add_fusion
  251.5 9.6 %multiply_reduce_fusion.2 = (f32[768]{0:T(1024)}, f32[1024]{0:T(1024)S(1)}, f32[1024,768]{0,1:T(8,128)S(1)}) fusion(f32[1024,768]{0,1:T(8,128)S(1)} %copy-done.20, f32[1024]{0:T(1024)S(1)} %fusion.68, f32[1024]{0:T(1024)S(1)} %broadcast_multiply_fusion.3, f32[768]{0:T(1024)S(1)} %copy-done.55, bf16[768,2304]{1,0:T(8,128)(2,1)} %all-gather.9.cloned.1.call-done, ...), kind=kOutput, calls=%fused_computation.76 | convolution fusion | flops 3634100480 | bytes 19286016 | tf_op jit(solution)/shard_map/tf,df->td/dot_general | solution.py:150
  264.8 2.9 fusion.51
  267.7 5.7 fusion.47
  273.5 3.3 convolution_convert_fusion
  279.3 9.1 %fusion.59 = f32[768,2304]{1,0:T(8,128)} fusion(f32[1024,1152]{1,0:T(8,128)S(1)} %bitcast.77, f32[1024,1152]{1,0:T(8,128)} %get-tuple-element.56, f32[1024,768]{0,1:T(8,128)S(1)} %copy-done.21, f32[768]{0:T(1024)S(1)} %copy-done.55, f32[1024]{0:T(1024)S(1)} %fusion.68, f32[1024]{0:T(1024)S(1)} %broadcast_multiply_fusion.3), kind=kOutput, calls=%fused_computation.113 | convolution fusion | flops 3631742976 | bytes 19672064 | tf_op jit(solution)/shard_map/td,tf->df/dot_general | solution.py:149
  289.5 18.0 %multiply_reduce_fusion.1 = (f32[12,512]{1,0:T(8,128)S(1)}, f32[12,512,1024]{2,1,0:T(8,128)}) fusion(f32[12,512]{1,0:T(8,128)S(1)} %log_add_fusion.1, f32[12,512,1024]{2,1,0:T(8,128)} %get-tuple-element.87, pred[512,1024]{1,0:T(8,128)(4,1)S(1)} %copy-done.14, bf16[512,12,64]{0,2,1:T(8,128)(2,1)} %bitcast.78, bf16[1024,12,64]{0,2,1:T(8,128)(2,1)S(1)} %bitcast.70), kind=kOutput, calls=%fused_computation.4 | convolution fusion | flops 836757504 | bytes 53264384 | tf_op jit(solution)/shard_map/qhd,khd->hqk/dot_general | solution.py:177
  307.4 17.8 %multiply_reduce_fusion = (f32[12,512]{1,0:T(8,128)S(1)}, f32[12,512,1024]{2,1,0:T(8,128)}) fusion(f32[12,512]{1,0:T(8,128)S(1)} %log_add_fusion, f32[12,512,1024]{2,1,0:T(8,128)} %get-tuple-element.85, pred[512,1024]{1,0:T(8,128)(4,1)S(1)} %copy-done.17, bf16[512,12,64]{0,2,1:T(8,128)(2,1)} %bitcast.80, bf16[1024,12,64]{0,2,1:T(8,128)(2,1)S(1)} %bitcast.71), kind=kOutput, calls=%fused_computation.1 | convolution fusion | flops 836757504 | bytes 53264384 | tf_op jit(solution)/shard_map/qhd,khd->hqk/dot_general | solution.py:177
  325.2 42.6 %multiply_convert_fusion = (bf16[12,512,1024]{2,1,0:T(8,128)(2,1)}, bf16[12,512,1024]{2,1,0:T(8,128)(2,1)}) fusion(f32[12,512,1024]{2,1,0:T(8,128)} %get-tuple-element.95, f32[12,512]{1,0:T(8,128)S(1)} %get-tuple-element.94, f32[12,512]{1,0:T(8,128)S(1)} %log_add_fusion, f32[12,512,1024]{2,1,0:T(8,128)} %get-tuple-element.85, ...), kind=kLoop, calls=%fused_computation | loop fusion | flops 75497472 | bytes 126976000 | tf_op jit(solution)/shard_map/convert_element_type | solution.py:181
  367.9 10.4 %convolution_multiply_fusion = f32[12,64,512]{2,1,0:T(8,128)} fusion(bf16[1024,12,64]{0,2,1:T(8,128)(2,1)} %copy-done.3, bf16[12,512,1024]{2,1,0:T(8,128)(2,1)} %get-tuple-element.100), kind=kOutput, calls=%fused_computation.99 | convolution fusion | flops 805699584 | bytes 15728640 | tf_op jit(solution)/shard_map/hqk,khd->qhd/dot_general | solution.py:183
  378.3 6.6 convolution_multiply_fusion.1
  384.9 2.3 maximum_multiply_fusion.3
  389.5 2.1 fusion.36
  391.6 2.3 fusion.55
  395.5 3.7 bitcast_multiply_fusion
  401.5 12.1 %fusion.4 = f32[12,64,1024]{2,1,0:T(8,128)S(1)} fusion(bf16[512,12,64]{0,2,1:T(8,128)(2,1)S(1)} %bitcast.81, f32[12,512]{1,0:T(8,128)S(1)} %log_add_fusion, f32[12,512,1024]{2,1,0:T(8,128)} %get-tuple-element.85, pred[512,1024]{1,0:T(8,128)(4,1)S(1)} %copy-done.18), kind=kOutput, calls=%fused_computation.16 | convolution fusion | flops 830472192 | bytes 29646848 | tf_op jit(solution)/shard_map/hqk,qhd->khd/dot_general | solution.py:174
  413.6 12.0 %add_convert_fusion.1 = bf16[12,64,1024]{2,1,0:T(8,128)(2,1)S(1)} fusion(f32[12,64,1024]{2,1,0:T(8,128)S(1)} %fusion.4, bf16[512,12,64]{0,2,1:T(8,128)(2,1)S(1)} %bitcast.79, f32[12,512]{1,0:T(8,128)S(1)} %log_add_fusion.1, f32[12,512,1024]{2,1,0:T(8,128)} %get-tuple-element.87, pred[512,1024]{1,0:T(8,128)(4,1)S(1)} %copy-done.15), kind=kOutput, calls=%fused_computation.78 | convolution fusion | flops 832045056 | bytes 31219712 | tf_op jit(solution)/shard_map/hqk,qhd->khd/dot_general | solution.py:174
  426.8 6.8 fusion.39
  436.1 13.5 %collective-permute-done = bf16[96,1152]{1,0:T(8,128)(2,1)} collective-permute-done((bf16[96,1152]{1,0:T(8,128)(2,1)S(1)}, bf16[96,1152]{1,0:T(8,128)(2,1)}, u32[]{:S(2)}, u32[]{:S(2)}) %collective-permute-start) | collective-permute-done | bytes 221216 | tf_op jit(solution)/shard_map/ppermute | solution.py:24
  450.5 14.0 %collective-permute-done.1 = bf16[96,1152]{1,0:T(8,128)(2,1)S(1)} collective-permute-done((bf16[96,1152]{1,0:T(8,128)(2,1)}, bf16[96,1152]{1,0:T(8,128)(2,1)S(1)}, u32[]{:S(2)}, u32[]{:S(2)}) %collective-permute-start.1) | collective-permute-done | bytes 221216 | tf_op jit(solution)/shard_map/ppermute | solution.py:24
  464.6 14.7 %collective-permute-done.2 = bf16[96,1152]{1,0:T(8,128)(2,1)S(1)} collective-permute-done((bf16[96,1152]{1,0:T(8,128)(2,1)S(1)}, bf16[96,1152]{1,0:T(8,128)(2,1)S(1)}, u32[]{:S(2)}, u32[]{:S(2)}) %collective-permute-start.2) | collective-permute-done | bytes 221216 | tf_op jit(solution)/shard_map/ppermute | solution.py:24
  479.3 14.2 %collective-permute-done.3 = bf16[96,1152]{1,0:T(8,128)(2,1)S(1)} collective-permute-done((bf16[96,1152]{1,0:T(8,128)(2,1)S(1)}, bf16[96,1152]{1,0:T(8,128)(2,1)S(1)}, u32[]{:S(2)}, u32[]{:S(2)}) %collective-permute-start.3) | collective-permute-done | bytes 221216 | tf_op jit(solution)/shard_map/ppermute | solution.py:24
  493.5 19.8 %collective-permute-done.4 = bf16[96,1152]{1,0:T(8,128)(2,1)S(1)} collective-permute-done((bf16[96,1152]{1,0:T(8,128)(2,1)S(1)}, bf16[96,1152]{1,0:T(8,128)(2,1)S(1)}, u32[]{:S(2)}, u32[]{:S(2)}) %collective-permute-start.4) | collective-permute-done | bytes 221216 | tf_op jit(solution)/shard_map/ppermute | solution.py:24
  513.4 8.7 %collective-permute-done.5 = bf16[96,1152]{1,0:T(8,128)(2,1)S(1)} collective-permute-done((bf16[96,1152]{1,0:T(8,128)(2,1)S(1)}, bf16[96,1152]{1,0:T(8,128)(2,1)S(1)}, u32[]{:S(2)}, u32[]{:S(2)}) %collective-permute-start.5) | collective-permute-done | bytes 221216 | tf_op jit(solution)/shard_map/ppermute | solution.py:24
  522.3 8.7 %collective-permute-done.6 = bf16[96,1152]{1,0:T(8,128)(2,1)S(1)} collective-permute-done((bf16[96,1152]{1,0:T(8,128)(2,1)S(1)}, bf16[96,1152]{1,0:T(8,128)(2,1)S(1)}, u32[]{:S(2)}, u32[]{:S(2)}) %collective-permute-start.6) | collective-permute-done | bytes 221216 | tf_op jit(solution)/shard_map/ppermute | solution.py:24
  531.0 5.5 fusion.30
  539.6 3.4 add_convert_fusion.2
  543.0 1.6 convert_element_type.166
  544.6 1.7 convert_element_type.170
  546.3 36.6 %reduce-scatter.9.cloned.1.call-done = f32[96,2304]{1,0:T(8,128)} async-done(((f32[768,2304]{1,0:T(8,128)}), f32[96,2304]{1,0:T(8,128)}) %reduce-scatter.9.cloned.1.call-update) | async-done | bytes 884752 | tf_op jit(solution)/shard_map/reduce_scatter | solution.py:212
  583.0 2.0 convert_element_type.168
  585.0 130.3 %reduce-scatter.5.cloned.1.call-done = f32[96,2304]{1,0:T(8,128)} async-done(((f32[768,2304]{1,0:T(8,128)}), f32[96,2304]{1,0:T(8,128)}) %reduce-scatter.5.cloned.1.call-update) | async-done | bytes 884752 | tf_op jit(solution)/shard_map/reduce_scatter | solution.py:210
  715.2 2.0 convert_element_type.164
  717.2 2.6 copy.55
  719.8 19.7 %all-reduce.6 = (bf16[768]{0:T(1024)(128)(2,1)S(1)}, bf16[768]{0:T(1024)(128)(2,1)S(1)}) all-reduce(f32[768]{0:T(1024)S(1)} %get-tuple-element.42, f32[768]{0:T(1024)S(1)} %copy-done.56), channel_id=6, replica_groups=mesh['fsdp'=8,'rep'=4] {'fsdp'}, use_global_device_ids=true, to_apply=%region_24.25.clone | all-reduce | flops 1536 | bytes 9216
  739.7 5.6 all-reduce.8
  746.3 6.1 add_add_fusion.2
  752.4 3.6 copy.56
  756.5 1.6 convert_element_type.167
  758.1 2.0 convert_element_type.165
  760.1 1.7 convert_element_type.171
  761.8 2.0 convert_element_type.169
  (229 shorter events, 45.1 us)
Async XLA Ops:
  7.2 36.7 %copy-start.34 = (bf16[1024,768]{1,0:T(8,128)(2,1)S(1)}, bf16[1024,768]{1,0:T(8,128)(2,1)}, u32[]{:S(2)}) copy-start(bf16[1024,768]{1,0:T(8,128)(2,1)} %param.10) | copy-start | bytes 4718596
  7.2 71.2 %all-gather.5.cloned.1.call-start = ((), (), s32[]{:S(2)}) async-start(), calls=%async_computation.4 | async-start | bytes 3981312 | tf_op jit(solution)/shard_map/all_gather | solution.py:90
  7.9 162.3 %all-gather.7.cloned.1.call-start = ((), (), s32[]{:S(2)}) async-start(), calls=%async_computation.5 | async-start | bytes 1327104 | tf_op jit(solution)/shard_map/all_gather | solution.py:91
  8.7 177.7 %all-gather.9.cloned.1.call-start = ((), (), s32[]{:S(2)}) async-start(), calls=%async_computation.6 | async-start | bytes 3981312 | tf_op jit(solution)/shard_map/all_gather | solution.py:92
  9.4 223.5 %all-gather.11.cloned.1.call-start = ((), (), s32[]{:S(2)}) async-start(), calls=%async_computation.7 | async-start | bytes 1990656 | tf_op jit(solution)/shard_map/all_gather | solution.py:137
  10.0 533.0 %reduce-scatter.7.cloned.1.call-start = ((), (), s32[]{:S(2)}) async-start(), calls=%async_computation.9 | async-start | bytes 2654208 | tf_op jit(solution)/shard_map/reduce_scatter | solution.py:211
  40.7 37.7 %copy-start.46 = (f32[768]{0:T(1024)}, f32[768]{0:T(1024)S(1)}, u32[]{:S(2)}) copy-start(f32[768]{0:T(1024)S(1)} %convert_element_type.135) | copy-start | bytes 9220
  43.9 57.2 %copy-start.29 = (f32[1024,64]{0,1:T(8,128)}, f32[1024,64]{0,1:T(8,128)S(1)}, u32[]{:S(2)}) copy-start(f32[1024,64]{0,1:T(8,128)S(1)} %get-tuple-element.77) | copy-start | bytes 786436
  44.7 125.6 %copy-start.1 = (bf16[1024,768]{0,1:T(8,128)(2,1)}, bf16[1024,768]{0,1:T(8,128)(2,1)S(1)}, u32[]{:S(2)}) copy-start(bf16[1024,768]{0,1:T(8,128)(2,1)S(1)} %copy.49) | copy-start | bytes 4718596
  44.7 3.6 copy-start.54
  45.0 39.6 %copy-start.42 = (f32[1024]{0:T(1024)}, f32[1024]{0:T(1024)S(1)}, u32[]{:S(2)}) copy-start(f32[1024]{0:T(1024)S(1)} %broadcast_multiply_fusion.4) | copy-start | bytes 12292
  46.6 38.0 %copy-start.48 = (f32[1024]{0:T(1024)}, f32[1024]{0:T(1024)S(1)}, u32[]{:S(2)}) copy-start(f32[1024]{0:T(1024)S(1)} %fusion.67) | copy-start | bytes 12292
  97.8 2.8 copy-start.5
  104.4 10.9 %copy-start.3 = (bf16[1024,12,64]{0,2,1:T(8,128)(2,1)}, bf16[1024,12,64]{0,2,1:T(8,128)(2,1)S(1)}, u32[]{:S(2)}) copy-start(bf16[1024,12,64]{0,2,1:T(8,128)(2,1)S(1)} %get-tuple-element.73) | copy-start | bytes 4718596
  104.4 10.9 %copy-start.7 = (bf16[1024,12,64]{0,2,1:T(8,128)(2,1)}, bf16[1024,12,64]{0,2,1:T(8,128)(2,1)S(1)}, u32[]{:S(2)}) copy-start(bf16[1024,12,64]{0,2,1:T(8,128)(2,1)S(1)} %get-tuple-element.72) | copy-start | bytes 4718596
  104.4 10.9 %copy-start.13 = (pred[512,1024]{1,0:T(8,128)(4,1)S(1)}, pred[512,1024]{1,0:T(8,128)(4,1)}, u32[]{:S(2)}) copy-start(pred[512,1024]{1,0:T(8,128)(4,1)} %get-tuple-element.78) | copy-start | bytes 1572868
  138.0 13.9 %slice-start = ((s8[25165824]{0:T(1024)(128)(4,1)}), s8[4194304]{0:T(1024)(128)(4,1)S(1)}, s32[]{:S(2)}) async-start(s8[25165824]{0:T(1024)(128)(4,1)} %bitcast.60), calls=%async_computation.13 | async-start | bytes 8388608
  138.0 13.9 %slice-start.1 = ((s8[25165824]{0:T(1024)(128)(4,1)}), s8[4194304]{0:T(1024)(128)(4,1)S(1)}, s32[]{:S(2)}) async-start(s8[25165824]{0:T(1024)(128)(4,1)} %bitcast.60), calls=%async_computation.14 | async-start | bytes 8388608
  138.0 13.8 %slice-start.2 = ((s8[25165824]{0:T(1024)(128)(4,1)}), s8[4194304]{0:T(1024)(128)(4,1)S(1)}, s32[]{:S(2)}) async-start(s8[25165824]{0:T(1024)(128)(4,1)} %bitcast.60), calls=%async_computation.15 | async-start | bytes 8388608
  138.0 13.8 %slice-start.3 = ((s8[25165824]{0:T(1024)(128)(4,1)}), s8[4194304]{0:T(1024)(128)(4,1)S(1)}, s32[]{:S(2)}) async-start(s8[25165824]{0:T(1024)(128)(4,1)} %bitcast.60), calls=%async_computation.16 | async-start | bytes 8388608
  138.1 14.7 %slice-start.4 = ((s8[25165824]{0:T(1024)(128)(4,1)}), s8[4194304]{0:T(1024)(128)(4,1)S(1)}, s32[]{:S(2)}) async-start(s8[25165824]{0:T(1024)(128)(4,1)} %bitcast.60), calls=%async_computation.17 | async-start | bytes 8388608
  138.1 16.2 %slice-start.5 = ((s8[25165824]{0:T(1024)(128)(4,1)}), s8[4194304]{0:T(1024)(128)(4,1)S(1)}, s32[]{:S(2)}) async-start(s8[25165824]{0:T(1024)(128)(4,1)} %bitcast.60), calls=%async_computation.18 | async-start | bytes 8388608
  173.5 12.9 %copy-start.55 = (f32[768]{0:T(1024)S(1)}, f32[768]{0:T(1024)}, u32[]{:S(2)}) copy-start(f32[768]{0:T(1024)} %convert_element_type.150) | copy-start | bytes 9220
  175.2 57.6 %copy-start.9 = (bf16[1024,768]{0,1:T(8,128)(2,1)S(1)}, bf16[1024,768]{0,1:T(8,128)(2,1)}, u32[]{:S(2)}) copy-start(bf16[1024,768]{0,1:T(8,128)(2,1)} %copy.54) | copy-start | bytes 4718596
  175.2 57.7 %copy-start.44 = (f32[1024]{0:T(1024)S(1)}, f32[1024]{0:T(1024)}, u32[]{:S(2)}) copy-start(f32[1024]{0:T(1024)} %convert_element_type.155) | copy-start | bytes 12292
  232.9 15.2 %copy-start.24 = (f32[1024,2304]{1,0:T(8,128)S(1)}, f32[1024,2304]{1,0:T(8,128)}, u32[]{:S(2)}) copy-start(f32[1024,2304]{1,0:T(8,128)} %fusion.83) | copy-start | bytes 28311556
  248.0 3.5 copy-start.20
  251.5 9.6 %copy-start.25 = (f32[1024,1152]{1,0:T(8,128)}, f32[1024,1152]{1,0:T(8,128)S(1)}, u32[]{:S(2)}) copy-start(f32[1024,1152]{1,0:T(8,128)S(1)} %get-tuple-element.58) | copy-start | bytes 14155780
  267.6 277.0 %reduce-scatter.11.cloned.1.call-start = ((), (), s32[]{:S(2)}) async-start(), calls=%async_computation.11 | async-start | bytes 3981312 | tf_op jit(solution)/shard_map/reduce_scatter | solution.py:213
  273.4 4.7 slice-start.9
  273.4 309.6 %reduce-scatter.9.cloned.1.call-start = ((), (), s32[]{:S(2)}) async-start(), calls=%async_computation.10 | async-start | bytes 7962624 | tf_op jit(solution)/shard_map/reduce_scatter | solution.py:212
  273.5 4.6 slice-start.10
  288.4 426.8 %reduce-scatter.5.cloned.1.call-start = ((), (), s32[]{:S(2)}) async-start(), calls=%async_computation.8 | async-start | bytes 7962624 | tf_op jit(solution)/shard_map/reduce_scatter | solution.py:210
  289.5 18.0 %copy-start.17 = (pred[512,1024]{1,0:T(8,128)(4,1)S(1)}, pred[512,1024]{1,0:T(8,128)(4,1)}, u32[]{:S(2)}) copy-start(pred[512,1024]{1,0:T(8,128)(4,1)} %get-tuple-element.79) | copy-start | bytes 1572868
  367.9 10.4 %copy-start = (bf16[12,512,1024]{2,1,0:T(8,128)(2,1)S(1)}, bf16[12,512,1024]{2,1,0:T(8,128)(2,1)}, u32[]{:S(2)}) copy-start(bf16[12,512,1024]{2,1,0:T(8,128)(2,1)} %get-tuple-element.101) | copy-start | bytes 37748740
  378.3 6.6 copy-start.32
  389.5 4.4 slice-start.6
  391.6 3.9 slice-start.8
  391.6 3.9 copy-start.28
  401.5 24.1 %copy-start.38 = (bf16[1024,12,64]{0,2,1:T(8,128)(2,1)}, bf16[1024,12,64]{0,2,1:T(8,128)(2,1)S(1)}, u32[]{:S(2)}) copy-start(bf16[1024,12,64]{0,2,1:T(8,128)(2,1)S(1)} %fusion.37) | copy-start | bytes 4718596
  401.5 12.1 %copy-start.15 = (pred[512,1024]{1,0:T(8,128)(4,1)S(1)}, pred[512,1024]{1,0:T(8,128)(4,1)}, u32[]{:S(2)}) copy-start(pred[512,1024]{1,0:T(8,128)(4,1)} %get-tuple-element.78) | copy-start | bytes 1572868
  401.5 12.1 %copy-start.26 = (bf16[512,768]{0,1:T(8,128)(2,1)S(1)}, bf16[512,768]{0,1:T(8,128)(2,1)}, u32[]{:S(2)}) copy-start(bf16[512,768]{0,1:T(8,128)(2,1)} %get-tuple-element.70) | copy-start | bytes 2359300
  413.6 13.2 %copy-start.2 = (bf16[1024,768]{0,1:T(8,128)(2,1)S(1)}, bf16[1024,768]{0,1:T(8,128)(2,1)}, u32[]{:S(2)}) copy-start(bf16[1024,768]{0,1:T(8,128)(2,1)} %copy-done.1) | copy-start | bytes 4718596
  413.6 13.2 %copy-start.37 = (bf16[1024,768]{0,1:T(8,128)(2,1)S(1)}, bf16[1024,768]{0,1:T(8,128)(2,1)}, u32[]{:S(2)}) copy-start(bf16[1024,768]{0,1:T(8,128)(2,1)} %fusion.36) | copy-start | bytes 4718596
  413.6 13.2 %copy-start.43 = (f32[1024]{0:T(1024)S(1)}, f32[1024]{0:T(1024)}, u32[]{:S(2)}) copy-start(f32[1024]{0:T(1024)} %copy-done.42) | copy-start | bytes 12292
  413.6 13.2 %copy-start.47 = (f32[768]{0:T(1024)S(1)}, f32[768]{0:T(1024)}, u32[]{:S(2)}) copy-start(f32[768]{0:T(1024)} %copy-done.46) | copy-start | bytes 9220
  413.6 13.2 %copy-start.49 = (f32[1024]{0:T(1024)S(1)}, f32[1024]{0:T(1024)}, u32[]{:S(2)}) copy-start(f32[1024]{0:T(1024)} %copy-done.48) | copy-start | bytes 12292
  433.6 322.9 %all-reduce.12.cloned.1.call-start = ((), (), s32[]{:S(2)}) async-start(), calls=%async_computation.12 | async-start | bytes 2506752 | tf_op jit(solution)/shard_map/psum | solution.py:218
  434.5 15.0 %collective-permute-start = (bf16[96,1152]{1,0:T(8,128)(2,1)S(1)}, bf16[96,1152]{1,0:T(8,128)(2,1)}, u32[]{:S(2)}, u32[]{:S(2)}) collective-permute-start(bf16[96,1152]{1,0:T(8,128)(2,1)S(1)} %copy-done.41), channel_id=1, source_target_pairs={{0,4},{4,8},{8,12},{12,16},{16,20},{20,24},{24,28},{28,0},{1,5},{5... | collective-permute-start | bytes 663560 | tf_op jit(solution)/shard_map/ppermute | solution.py:24
  435.9 95.1 %copy-start.39 = (bf16[1024,12,64]{0,2,1:T(8,128)(2,1)S(1)}, bf16[1024,12,64]{0,2,1:T(8,128)(2,1)}, u32[]{:S(2)}) copy-start(bf16[1024,12,64]{0,2,1:T(8,128)(2,1)} %copy-done.38) | copy-start | bytes 4718596
  435.9 95.1 %copy-start.57 = (bf16[768,2304]{1,0:T(8,128)(2,1)S(1)}, bf16[768,2304]{1,0:T(8,128)(2,1)}, u32[]{:S(2)}) copy-start(bf16[768,2304]{1,0:T(8,128)(2,1)} %all-gather.5.cloned.1.call-done) | copy-start | bytes 10616836
  449.5 15.0 %collective-permute-start.1 = (bf16[96,1152]{1,0:T(8,128)(2,1)}, bf16[96,1152]{1,0:T(8,128)(2,1)S(1)}, u32[]{:S(2)}, u32[]{:S(2)}) collective-permute-start(bf16[96,1152]{1,0:T(8,128)(2,1)} %collective-permute-done), channel_id=1, source_target_pairs={{0,4},{4,8},{8,12},{12,16},{16,20},{20,24},{24,28},{28,0},{1,5},{5... | collective-permute-start | bytes 663560 | tf_op jit(solution)/shard_map/ppermute | solution.py:24
  464.6 14.7 %collective-permute-start.2 = (bf16[96,1152]{1,0:T(8,128)(2,1)S(1)}, bf16[96,1152]{1,0:T(8,128)(2,1)S(1)}, u32[]{:S(2)}, u32[]{:S(2)}) collective-permute-start(bf16[96,1152]{1,0:T(8,128)(2,1)S(1)} %collective-permute-done.1), channel_id=1, source_target_pairs={{0,4},{4,8},{8,12},{12,16},{16,20},{20,24},{24,28},{28,0},{1,5},{5... | collective-permute-start | bytes 663560 | tf_op jit(solution)/shard_map/ppermute | solution.py:24
  479.3 14.2 %collective-permute-start.3 = (bf16[96,1152]{1,0:T(8,128)(2,1)S(1)}, bf16[96,1152]{1,0:T(8,128)(2,1)S(1)}, u32[]{:S(2)}, u32[]{:S(2)}) collective-permute-start(bf16[96,1152]{1,0:T(8,128)(2,1)S(1)} %collective-permute-done.2), channel_id=1, source_target_pairs={{0,4},{4,8},{8,12},{12,16},{16,20},{20,24},{24,28},{28,0},{1,5},{5... | collective-permute-start | bytes 663560 | tf_op jit(solution)/shard_map/ppermute | solution.py:24
  493.5 19.9 %collective-permute-start.4 = (bf16[96,1152]{1,0:T(8,128)(2,1)S(1)}, bf16[96,1152]{1,0:T(8,128)(2,1)S(1)}, u32[]{:S(2)}, u32[]{:S(2)}) collective-permute-start(bf16[96,1152]{1,0:T(8,128)(2,1)S(1)} %collective-permute-done.3), channel_id=1, source_target_pairs={{0,4},{4,8},{8,12},{12,16},{16,20},{20,24},{24,28},{28,0},{1,5},{5... | collective-permute-start | bytes 663560 | tf_op jit(solution)/shard_map/ppermute | solution.py:24
  513.3 8.7 %collective-permute-start.5 = (bf16[96,1152]{1,0:T(8,128)(2,1)S(1)}, bf16[96,1152]{1,0:T(8,128)(2,1)S(1)}, u32[]{:S(2)}, u32[]{:S(2)}) collective-permute-start(bf16[96,1152]{1,0:T(8,128)(2,1)S(1)} %collective-permute-done.4), channel_id=1, source_target_pairs={{0,4},{4,8},{8,12},{12,16},{16,20},{20,24},{24,28},{28,0},{1,5},{5... | collective-permute-start | bytes 663560 | tf_op jit(solution)/shard_map/ppermute | solution.py:24
  522.1 8.9 %collective-permute-start.6 = (bf16[96,1152]{1,0:T(8,128)(2,1)S(1)}, bf16[96,1152]{1,0:T(8,128)(2,1)S(1)}, u32[]{:S(2)}, u32[]{:S(2)}) collective-permute-start(bf16[96,1152]{1,0:T(8,128)(2,1)S(1)} %collective-permute-done.5), channel_id=1, source_target_pairs={{0,4},{4,8},{8,12},{12,16},{16,20},{20,24},{24,28},{28,0},{1,5},{5... | collective-permute-start | bytes 663560 | tf_op jit(solution)/shard_map/ppermute | solution.py:24
  531.0 5.5 copy-start.53
  531.0 8.5 %copy-start.33 = (bf16[1024,1152]{1,0:T(8,128)(2,1)S(1)}, bf16[1024,1152]{1,0:T(8,128)(2,1)}, u32[]{:S(2)}) copy-start(bf16[1024,1152]{1,0:T(8,128)(2,1)} %get-tuple-element.59) | copy-start | bytes 7077892
  536.5 3.1 copy-start.22
  584.9 134.9 %copy-start.56 = (f32[768]{0:T(1024)S(1)}, f32[768]{0:T(1024)}, u32[]{:S(2)}) copy-start(f32[768]{0:T(1024)} %get-tuple-element.40) | copy-start | bytes 9220
  584.9 161.4 %copy-start.10 = (bf16[1024,768]{0,1:T(8,128)(2,1)S(1)}, bf16[1024,768]{0,1:T(8,128)(2,1)}, u32[]{:S(2)}) copy-start(bf16[1024,768]{0,1:T(8,128)(2,1)} %copy.54) | copy-start | bytes 4718596
  585.0 161.4 %copy-start.45 = (f32[1024]{0:T(1024)S(1)}, f32[1024]{0:T(1024)}, u32[]{:S(2)}) copy-start(f32[1024]{0:T(1024)} %convert_element_type.155) | copy-start | bytes 12292
  585.0 161.4 %copy-start.51 = (f32[1024]{0:T(1024)S(1)}, f32[1024]{0:T(1024)}, u32[]{:S(2)}) copy-start(f32[1024]{0:T(1024)} %copy-done.50) | copy-start | bytes 12292
  (24 other events, 41.0 us)
Sparse Core Ops, SparseCore 0:
  10.2 68.1 all-gather.4
  80.6 39.5 all-gather.6
  122.4 63.9 all-gather.8
  188.4 44.3 all-gather.10
  267.8 68.0 reduce-scatter.6
  339.3 78.1 reduce-scatter.10
  421.2 161.7 reduce-scatter.8
  587.1 128.0 reduce-scatter.4
  718.4 38.0 all-reduce.11
